TPU v7x, 1024 devices: a whole 8x8x8 slice. The times are simulated.
1024 devices in a mesh: dp: 16 (over x, core), expert: 64 (over z, y).
Axes of the slice: x: 8, y: 8, z: 8, core: 2. Of those that a mesh axis runs over, the one named last changes fastest.
Arguments:
- tokens: bfloat16 [2048, 7168], P('dp', 'expert'), may hold values from -6 to 6
- routes: int32 [2048, 4], P('dp'), may hold values from 0 to 127, all different within a row; in each aligned block of 128 rows (0 to 127, 128 to 255, ...) at most 12 rows name the same one
- scores: int32 [2048, 4], P('dp'), may hold values from 1 to 16
- down_proj: bfloat16 [7168, 1024], P('expert'), may hold values from -0.0625 to 0.0625
- up_proj: bfloat16 [1024, 7168], P(None, 'expert'), may hold values from -0.1875 to 0.1875
- expert_gate: bfloat16 [1024, 262144], P(None, ('dp', 'expert')), may hold values from -0.1875 to 0.1875
- expert_up: bfloat16 [1024, 262144], P(None, ('dp', 'expert')), may hold values from -0.1875 to 0.1875
- expert_down: bfloat16 [262144, 1024], P(('dp', 'expert')), may hold values from -0.125 to 0.125
- cotangent: bfloat16 [2048, 7168], P('dp', 'expert'), may hold values from -12 to 12
Outputs:
- layer_out: bfloat16 [2048, 7168], P('dp', 'expert')
- token_grad: bfloat16 [2048, 7168], P('dp', 'expert')
- down_grad: float32 [7168, 1024], P('expert', 'dp')
- up_grad: float32 [1024, 7168], P('dp', 'expert')
- expert_gate_grad: bfloat16 [1024, 262144], P(None, ('dp', 'expert'))
- expert_up_grad: bfloat16 [1024, 262144], P(None, ('dp', 'expert'))
- expert_down_grad: bfloat16 [262144, 1024], P(('dp', 'expert'))
Inputs may be any that keep to these rules, and one draw needn't show every extreme that they name: `routes`: each row names 4 different experts. Within the 128 tokens of one index of dp no expert is named by more than 12 rows, a bound that some block reaches.
All inputs are finite; a program needn't handle non-finite values.
Results may differ from a plain program's by a relative error of at most 0.025.
Values may be sent and summed in bfloat16 or wider, within the bound.
A program may use at most 32 MiB of HBM per device.

v0:
```python
import jax
import jax.numpy as jnp
from jax import lax
from jax.sharding import PartitionSpec as P

exact_mode = lax.Precision.HIGHEST


def local(
    tokens, routes, scores, down_proj, up_proj, expert_gate, expert_up, expert_down, cotangent
):
    row_total = lax.axis_size("dp")
    col_total = lax.axis_size("expert")
    tok_row = tokens.shape[0]
    chosen = routes.shape[1]
    tok_share = tok_row // col_total
    capacity = min(96 * tok_share // row_total, tok_row)
    my_col = lax.axis_index("expert")
    targets = (jnp.arange(row_total, dtype=jnp.int32) * col_total + my_col) // 8
    matches = (routes[None, :, :] == targets[:, None, None]).astype(jnp.int32)
    flat_match = matches.reshape(row_total, tok_row * chosen)
    before = jnp.cumsum(flat_match, axis=1, dtype=jnp.int32) - flat_match
    places = jnp.arange(capacity, dtype=jnp.int32)
    onehot = ((before[:, :, None] == places[None, None, :]) & (flat_match[:, :, None] > 0)).astype(
        jnp.float32
    )
    onehot = onehot.reshape(row_total, tok_row, chosen, capacity)
    score_vals = scores.astype(jnp.float32)
    share = score_vals / jnp.sum(score_vals, axis=1, keepdims=True)
    picker = jnp.einsum("rtkp->rpt", onehot)
    weighted = jnp.einsum("rtkp,tk->rpt", onehot, share, precision=exact_mode)
    picker_low = picker.astype(jnp.bfloat16)

    def column_total(term_fn):
        whole = lax.psum(term_fn(0, tok_row), "expert")
        result = whole.astype(jnp.bfloat16)
        return result

    def to_experts(outgoing):
        return lax.all_to_all(outgoing, "dp", split_axis=0, concat_axis=0, tiled=True)

    def from_experts(outgoing):
        return lax.all_to_all(
            outgoing.astype(jnp.bfloat16), "dp", split_axis=0, concat_axis=0, tiled=True
        ).astype(outgoing.dtype)

    def latent_term(offset, number):
        return jnp.dot(tokens, down_proj, preferred_element_type=jnp.float32)

    latent = column_total(latent_term)
    outgoing = jnp.einsum(
        "rpt,tl->rpl", picker_low, latent, preferred_element_type=jnp.float32
    ).astype(jnp.bfloat16)
    arrived = to_experts(outgoing)
    slot_rows = arrived.reshape(row_total * capacity, arrived.shape[2])
    gate_val = jnp.dot(slot_rows, expert_gate, preferred_element_type=jnp.float32)
    lift_val = jnp.dot(slot_rows, expert_up, preferred_element_type=jnp.float32)
    sigma_val = jax.nn.sigmoid(gate_val)
    active = gate_val * sigma_val
    hidden = (active * lift_val).astype(jnp.bfloat16)
    partial_value = jnp.dot(hidden, expert_down, preferred_element_type=jnp.float32)
    returned = from_experts(partial_value.reshape(row_total, capacity, partial_value.shape[1]))

    def combine_term(offset, number):
        return jnp.einsum("rpt,rpl->tl", weighted, returned, precision=exact_mode)

    combined = column_total(combine_term)
    layer_out = jnp.dot(combined, up_proj, preferred_element_type=jnp.float32).astype(jnp.bfloat16)

    def grad_term(offset, number):
        return jnp.dot(cotangent, up_proj.T, preferred_element_type=jnp.float32)

    combined_grad = column_total(grad_term)
    up_part = jnp.dot(combined.T, cotangent, preferred_element_type=jnp.float32)
    route_grad = jnp.einsum(
        "rpt,tl->rpl", weighted, combined_grad.astype(jnp.float32), precision=exact_mode
    ).astype(jnp.bfloat16)
    grad_arrived = to_experts(route_grad)
    grad_rows = grad_arrived.reshape(row_total * capacity, grad_arrived.shape[2])
    hidden_grad = jnp.dot(grad_rows, expert_down.T, preferred_element_type=jnp.float32)
    gate_grad = (
        hidden_grad * lift_val * (sigma_val * (1.0 + gate_val * (1.0 - sigma_val)))
    ).astype(jnp.bfloat16)
    lift_grad = (hidden_grad * active).astype(jnp.bfloat16)
    latent_part = jnp.dot(gate_grad, expert_gate.T, preferred_element_type=jnp.float32) + jnp.dot(
        lift_grad, expert_up.T, preferred_element_type=jnp.float32
    )
    latent_back = from_experts(latent_part.reshape(row_total, capacity, latent_part.shape[1]))

    def back_term(offset, number):
        return jnp.einsum("rpt,rpl->tl", picker, latent_back, precision=exact_mode)

    latent_grad = column_total(back_term)
    token_grad = jnp.dot(latent_grad, down_proj.T, preferred_element_type=jnp.float32).astype(
        jnp.bfloat16
    )
    down_part = jnp.dot(tokens.T, latent_grad, preferred_element_type=jnp.float32)
    up_grad, down_grad = (
        lax.psum_scatter(
            up_part.astype(jnp.bfloat16), "dp", scatter_dimension=0, tiled=True
        ).astype(jnp.float32),
        lax.psum_scatter(
            down_part.astype(jnp.bfloat16), "dp", scatter_dimension=1, tiled=True
        ).astype(jnp.float32),
    )
    expert_gate_grad = jnp.dot(slot_rows.T, gate_grad, preferred_element_type=jnp.float32).astype(
        jnp.bfloat16
    )
    expert_up_grad = jnp.dot(slot_rows.T, lift_grad, preferred_element_type=jnp.float32).astype(
        jnp.bfloat16
    )
    expert_down_grad = jnp.dot(hidden.T, grad_rows, preferred_element_type=jnp.float32).astype(
        jnp.bfloat16
    )
    return (
        layer_out,
        token_grad,
        down_grad,
        up_grad,
        expert_gate_grad,
        expert_up_grad,
        expert_down_grad,
    )


def solution(mesh):
    in_specs = (
        P("dp", "expert"),
        P("dp", None),
        P("dp", None),
        P("expert", None),
        P(None, "expert"),
        P(None, ("dp", "expert")),
        P(None, ("dp", "expert")),
        P(("dp", "expert"), None),
        P("dp", "expert"),
    )
    out_specs = (
        P("dp", "expert"),
        P("dp", "expert"),
        P("expert", "dp"),
        P("dp", "expert"),
        P(None, ("dp", "expert")),
        P(None, ("dp", "expert")),
        P(("dp", "expert"), None),
    )
    return jax.shard_map(local, mesh=mesh, in_specs=in_specs, out_specs=out_specs, check_vma=False)
```

profile of v0, /device:TPU:1, one launch (start us, length us, event | category | flops | bytes accessed | tf_op | source)
XLA Modules:
  0.0 810.5 jit_solution(5015058075181265077)
XLA Ops:
  8.2 1.1 reduce-window.6
  12.3 248.0 %all-reduce.4 = (bf16[128,1024]{1,0:T(8,128)(2,1)S(1)}, bf16[128,1024]{1,0:T(8,128)(2,1)S(1)}) all-reduce(f32[128,1024]{1,0:T(8,128)S(1)} %fusion.21, f32[128,1024]{1,0:T(8,128)S(1)} %fusion.23), channel_id=1, replica_groups=mesh['dp'=16,'expert'=64] {'expert'}, use_global_device_ids=true, to_apply=%region_4.5 | all-reduce | flops 262144 | bytes 1572864 | tf_op jit(solution)/shard_map/psum | solution.py:35
  260.6 1.0 copy.55
  261.6 62.5 %all-to-all-start = ((bf16[16,12,1024]{2,1,0:T(8,128)(2,1)}), bf16[16,12,1024]{2,1,0:T(8,128)(2,1)S(1)}, u32[]{:S(2)}, u32[]{:S(2)}) async-start(bf16[16,12,1024]{2,1,0:T(8,128)(2,1)} %copy.55), calls=%async_computation | async-start | bytes 1048576 | tf_op jit(solution)/shard_map/all_to_all | solution.py:40
  324.8 1.0 copy.57
  325.9 15.5 %all-to-all-done = bf16[16,12,1024]{2,1,0:T(8,128)(2,1)S(1)} async-done(((bf16[16,12,1024]{2,1,0:T(8,128)(2,1)}), bf16[16,12,1024]{2,1,0:T(8,128)(2,1)S(1)}, u32[]{:S(2)}, u32[]{:S(2)}) %all-to-all-start) | async-done | bytes 393248 | tf_op jit(solution)/shard_map/all_to_all | solution.py:40
  341.4 3.5 all-to-all-start.2
  345.0 0.9 copy-done.2
  346.2 15.4 %all-to-all-done.2 = bf16[16,12,1024]{2,1,0:T(8,128)(2,1)S(1)} async-done(((bf16[16,12,1024]{2,1,0:T(8,128)(2,1)}), bf16[16,12,1024]{2,1,0:T(8,128)(2,1)S(1)}, u32[]{:S(2)}, u32[]{:S(2)}) %all-to-all-start.2) | async-done | bytes 393248 | tf_op jit(solution)/shard_map/all_to_all | solution.py:40
  363.3 0.9 convert_element_type.114
  364.2 3.5 all-to-all-start.3
  367.9 0.9 convert_element_type.106
  368.8 15.6 %all-to-all-done.3 = bf16[16,12,1024]{2,1,0:T(8,128)(2,1)S(1)} async-done(((bf16[16,12,1024]{2,1,0:T(8,128)(2,1)}), bf16[16,12,1024]{2,1,0:T(8,128)(2,1)S(1)}, u32[]{:S(2)}, u32[]{:S(2)}) %all-to-all-start.3) | async-done | bytes 393248 | tf_op jit(solution)/shard_map/all_to_all | solution.py:43
  384.4 3.5 all-to-all-start.1
  387.9 1.1 convolution_convert_fusion.1
  389.1 1.1 convolution_convert_fusion.2
  390.8 13.8 %all-to-all-done.1 = bf16[16,12,1024]{2,1,0:T(8,128)(2,1)S(1)} async-done(((bf16[16,12,1024]{2,1,0:T(8,128)(2,1)}), bf16[16,12,1024]{2,1,0:T(8,128)(2,1)S(1)}, u32[]{:S(2)}, u32[]{:S(2)}) %all-to-all-start.1) | async-done | bytes 393248 | tf_op jit(solution)/shard_map/all_to_all | solution.py:43
  405.2 227.5 %all-reduce.5 = (bf16[128,1024]{1,0:T(8,128)(2,1)S(1)}, bf16[128,1024]{1,0:T(8,128)(2,1)S(1)}) all-reduce(f32[128,1024]{1,0:T(8,128)S(1)} %convolution_bitcast_fusion, f32[128,1024]{1,0:T(8,128)S(1)} %convolution_bitcast_fusion.1), channel_id=1, replica_groups=mesh['dp'=16,'expert'=64] {'expert'}, use_global_device_ids=true, to_apply=%region_7.8 | all-reduce | flops 262144 | bytes 1572864 | tf_op jit(solution)/shard_map/psum | solution.py:35
  634.7 1.1 convolution_convert_fusion
  635.8 1.0 convolution_convert_fusion.6
  636.8 0.9 copy-done.4
  639.5 98.3 %reduce-scatter.7.cloned.1.call-done = bf16[64,112]{1,0:T(8,128)(2,1)} async-done(((bf16[1024,112]{1,0:T(8,128)(2,1)}), bf16[64,112]{1,0:T(8,128)(2,1)}) %reduce-scatter.7.cloned.1.call-update) | async-done | bytes 14352
  739.4 63.0 %reduce-scatter.5.cloned.1.call-done = bf16[64,112]{1,0:T(8,128)(2,1)} async-done(((bf16[1024,112]{1,0:T(8,128)(2,1)}), bf16[64,112]{1,0:T(8,128)(2,1)}) %reduce-scatter.5.cloned.1.call-update) | async-done | bytes 14352 | tf_op jit(solution)/shard_map/reduce_scatter | solution.py:99
  802.3 1.3 convert_element_type.121
  (82 shorter events, 13.6 us)
Async XLA Ops:
  7.2 354.9 %copy-start = (bf16[1024,256]{1,0:T(8,128)(2,1)S(1)}, bf16[1024,256]{1,0:T(8,128)(2,1)}, u32[]{:S(2)}) copy-start(bf16[1024,256]{1,0:T(8,128)(2,1)} %param.15) | copy-start | bytes 1572868
  9.5 0.9 copy-start.3
  10.1 0.8 copy-start.15
  10.9 0.9 copy-start.5
  10.9 0.9 copy-start.17
  12.2 248.1 %copy-start.9 = (f32[16,128,12]{1,0,2:T(8,128)}, f32[16,128,12]{1,0,2:T(8,128)S(1)}, u32[]{:S(2)}) copy-start(f32[16,128,12]{1,0,2:T(8,128)S(1)} %convert_reduce_fusion) | copy-start | bytes 294916
  261.6 62.5 %copy-start.20 = (s32[128,4]{0,1:T(4,128)S(1)}, s32[128,4]{0,1:T(4,128)}, u32[]{:S(2)}) copy-start(s32[128,4]{0,1:T(4,128)} %param.11) | copy-start | bytes 6148
  261.6 79.8 %all-to-all-start = ((bf16[16,12,1024]{2,1,0:T(8,128)(2,1)}), bf16[16,12,1024]{2,1,0:T(8,128)(2,1)S(1)}, u32[]{:S(2)}, u32[]{:S(2)}) async-start(bf16[16,12,1024]{2,1,0:T(8,128)(2,1)} %copy.55), calls=%async_computation | async-start | bytes 1048576 | tf_op jit(solution)/shard_map/all_to_all | solution.py:40
  341.4 20.2 %all-to-all-start.2 = ((bf16[16,12,1024]{2,1,0:T(8,128)(2,1)}), bf16[16,12,1024]{2,1,0:T(8,128)(2,1)S(1)}, u32[]{:S(2)}, u32[]{:S(2)}) async-start(bf16[16,12,1024]{2,1,0:T(8,128)(2,1)} %copy.57), calls=%async_computation.2 | async-start | bytes 1048576 | tf_op jit(solution)/shard_map/all_to_all | solution.py:40
  344.9 1.0 copy-start.2
  346.2 15.5 %copy-start.1 = (bf16[256,1024]{1,0:T(8,128)(2,1)S(1)}, bf16[256,1024]{1,0:T(8,128)(2,1)}, u32[]{:S(2)}) copy-start(bf16[256,1024]{1,0:T(8,128)(2,1)} %param.16) | copy-start | bytes 1572868
  362.3 5.3 copy-start.11
  364.2 20.2 %all-to-all-start.3 = ((bf16[16,12,1024]{2,1,0:T(8,128)(2,1)}), bf16[16,12,1024]{2,1,0:T(8,128)(2,1)S(1)}, u32[]{:S(2)}, u32[]{:S(2)}) async-start(bf16[16,12,1024]{2,1,0:T(8,128)(2,1)} %convert_element_type.114), calls=%async_computation.3 | async-start | bytes 1048576 | tf_op jit(solution)/shard_map/all_to_all | solution.py:43
  384.4 20.2 %all-to-all-start.1 = ((bf16[16,12,1024]{2,1,0:T(8,128)(2,1)}), bf16[16,12,1024]{2,1,0:T(8,128)(2,1)S(1)}, u32[]{:S(2)}, u32[]{:S(2)}) async-start(bf16[16,12,1024]{2,1,0:T(8,128)(2,1)} %convert_element_type.106), calls=%async_computation.1 | async-start | bytes 1048576 | tf_op jit(solution)/shard_map/all_to_all | solution.py:43
  387.9 1.2 copy-start.14
  387.9 349.9 %reduce-scatter.7.cloned.1.call-start = ((), (), s32[]{:S(2)}) async-start(), calls=%async_computation.7 | async-start | bytes 278528
  389.1 1.2 copy-start.10
  390.2 14.4 %copy-start.8 = (f32[128,16,12]{0,1,2:T(8,128)S(1)}, f32[128,16,12]{0,1,2:T(8,128)}, u32[]{:S(2)}) copy-start(f32[128,16,12]{0,1,2:T(8,128)} %copy-done.7) | copy-start | bytes 294916
  405.2 227.5 %copy-start.16 = (bf16[128,112]{0,1:T(8,128)(2,1)S(1)}, bf16[128,112]{0,1:T(8,128)(2,1)}, u32[]{:S(2)}) copy-start(bf16[128,112]{0,1:T(8,128)(2,1)} %param.9) | copy-start | bytes 86020
  633.8 0.9 copy-start.12
  633.8 2.0 copy-start.18
  633.8 168.5 %reduce-scatter.5.cloned.1.call-start = ((), (), s32[]{:S(2)}) async-start(), calls=%async_computation.6 | async-start | bytes 278528 | tf_op jit(solution)/shard_map/reduce_scatter | solution.py:99
  636.7 0.9 copy-start.4
  637.7 0.9 copy-start.6
  (3 other events, 2.0 us)
Sparse Core Ops, SparseCore 0:
  633.9 103.8 reduce-scatter.6
  741.6 60.7 reduce-scatter.4
where the time goes:
time: 811 us
  blocking collectives  476 us (59%)
  waiting for transfers between devices  222 us (27%)
  starting transfers between devices  73 us (9%)
  between operations  14.4 us (2%)
  local copies, waits for them, and re-layouts  12.7 us (2%)
  matrix products  10.4 us (1%)
    psum x2, blocking collectives, column_total(): whole = lax.psum(term_fn(0, tok_row), 'expert')  476 us
    unnamed x3, waiting for transfers between devices  98.4 us
    all_to_all x2, starting transfers between devices, to_experts(): lax.all_to_all(outgoing, 'dp', split_axis=0, concat_axis=0, tiled=True)  65.9 us
    reduce_scatter x1, waiting for transfers between devices, local(): lax.psum_scatter(up_part.astype(jnp.bfloat16), 'dp', scatter_dimension=0,...  63 us
    all_to_all x2, waiting for transfers between devices, to_experts(): lax.all_to_all(outgoing, 'dp', split_axis=0, concat_axis=0, tiled=True)  30.9 us
    all_to_all x2, waiting for transfers between devices, from_experts(): lax.all_to_all(outgoing.astype(jnp.bfloat16), 'dp', split_axis=0, concat_...  29.4 us
  transfers between devices with their start and end apart: 6, of which 6 were waited for; matrix products, arithmetic and copies ran while one was open for 1% of the time, Pallas kernels for 0%

commit v1 on v0

v1 whole, which is shorter than its diff:
```python
import functools

import jax
import jax.numpy as jnp
from jax import lax
from jax.experimental import pallas as pl
from jax.experimental.pallas import tpu as pltpu
from jax.sharding import PartitionSpec as P

MESH = pl.DeviceIdType.MESH
BF = jnp.bfloat16
F32 = jnp.float32
NY = 8
CAP = 12
PAD = 16
LANE = 128


def nn(a, b):
    return jnp.dot(a, b, preferred_element_type=F32)


def nt(a, b):
    return lax.dot_general(a, b, (((1,), (1,)), ((), ())), preferred_element_type=F32)


def tn(a, b):
    return lax.dot_general(a, b, (((0,), (0,)), ((), ())), preferred_element_type=F32)


def kernel(
    ndp, nz, ny,
    tokens, routes, scores, down, up, w_gate, w_up, w_down, cot,
    layer_out, token_grad, down_grad, up_grad, gate_out, lift_out, dexp_out,
    f1, f1r, f2, f2r, b1, b1r, b2, b2r, low,
    pick, wpick, send4, recv4, full, ystage, yrecv, own, back, backr,
    z1, z1r, cf1, cb1, cf, cb, padc, padt, g1, g1r, g2, g2r,
    ssem, rsem, ysend, yrcv, psend, prcv,
):
    dp = lax.axis_index("dp")
    ex = lax.axis_index("expert")
    z, y = ex // ny, ex % ny
    xi, core = dp // 2, dp % 2
    nx = ndp // 2
    tok = tokens.shape[0]
    wide = tokens.shape[1]
    latent = down.shape[1]
    rows = tok // nz
    slots = ndp * PAD
    packed = ndp * CAP
    part = latent // ndp

    def ypeer(d):
        return (dp, z * ny + (y + d + ny) % ny)

    def zpeer(d):
        return (dp, ((z + d + nz) % nz) * ny + y)

    def dpeer(d):
        return ((dp + d + ndp) % ndp, ex)

    def xpeer(d):
        return (((xi + d + nx) % nx) * 2 + core, ex)

    sibling = (xi * 2 + 1 - core, ex)

    pending = []

    def send(src, dst, phase, device):
        pltpu.make_async_remote_copy(
            src_ref=src, dst_ref=dst, send_sem=ssem.at[phase], recv_sem=rsem.at[phase],
            device_id=device, device_id_type=MESH,
        ).start()

    def landed(ref, phase):
        pltpu.make_async_remote_copy(
            src_ref=ref, dst_ref=ref, send_sem=ssem.at[phase], recv_sem=rsem.at[phase],
            device_id=sibling, device_id_type=MESH,
        ).wait_recv()
        pending.append((ref, phase))

    barrier = pltpu.get_barrier_semaphore()
    for d in range(1, ny):
        pl.semaphore_signal(barrier, inc=1, device_id=ypeer(d), device_id_type=MESH)
    for d in range(1, nz):
        pl.semaphore_signal(barrier, inc=1, device_id=zpeer(d), device_id_type=MESH)
    for d in range(1, ndp):
        pl.semaphore_signal(barrier, inc=1, device_id=dpeer(d), device_id_type=MESH)

    part_f = nn(tokens[...], down[...]).astype(BF)
    for q in range(ny):
        f1[q] = part_f[:, q * LANE:(q + 1) * LANE]
    part_b = nt(cot[...], up[...]).astype(BF)
    for q in range(nz):
        b1[q] = part_b[q * rows:(q + 1) * rows]
    pl.semaphore_wait(barrier, ny + nz + ndp - 3)

    for d in range(1, ny):
        send(f1.at[(y + d) % ny], f1r.at[d], 0, ypeer(d))
    for d in range(1, nz):
        send(b1.at[(z + d) % nz], b1r.at[d], 1, zpeer(d))

    r = routes[...]
    s = scores[...].astype(F32)
    share = s / jnp.sum(s, axis=0, keepdims=True)
    target = ((lax.broadcasted_iota(jnp.int32, (ndp, tok), 0) + dp) % ndp) * nz + z
    member = jnp.zeros((ndp, tok), F32)
    weight = jnp.zeros((ndp, tok), F32)
    for k in range(r.shape[0]):
        hit = r[k:k + 1] == target
        member = member + jnp.where(hit, 1.0, 0.0)
        weight = weight + jnp.where(hit, share[k:k + 1], 0.0)
    ahead = lax.broadcasted_iota(jnp.int32, (tok, tok), 0) < lax.broadcasted_iota(jnp.int32, (tok, tok), 1)
    place = nn(member.astype(BF), jnp.where(ahead, 1.0, 0.0).astype(BF))
    place = jnp.where(member > 0.5, place, -1.0).astype(jnp.int32)
    spot = lax.broadcasted_iota(jnp.int32, (PAD, tok), 0)
    for d in range(ndp):
        hit = place[d:d + 1] == spot
        pick[d * PAD:(d + 1) * PAD] = jnp.where(hit, 1.0, 0.0).astype(BF)
        wpick[d * PAD:(d + 1) * PAD] = jnp.where(hit, weight[d:d + 1], 0.0).astype(BF)
    row = lax.broadcasted_iota(jnp.int32, (packed, slots), 0)
    col = lax.broadcasted_iota(jnp.int32, (packed, slots), 1)
    pack = jnp.where((col - row == (PAD - CAP) * (col // PAD)) & (col % PAD < CAP), 1.0, 0.0).astype(BF)
    row = lax.broadcasted_iota(jnp.int32, (slots, packed), 0)
    col = lax.broadcasted_iota(jnp.int32, (slots, packed), 1)
    unpack = jnp.where((row - col == (PAD - CAP) * (row // PAD)) & (row % PAD < CAP), 1.0, 0.0).astype(BF)

    landed(f1r.at[pl.ds(1, ny - 1)], 0)
    total = f1[y].astype(F32)
    for d in range(1, ny):
        total = total + f1r[d].astype(F32)
    total = total.astype(BF)
    for q in range(nz):
        f2[q] = total[q * rows:(q + 1) * rows]
    for d in range(1, nz):
        send(f2.at[(z + d) % nz], f2r.at[d], 2, zpeer(d))
    landed(b1r.at[pl.ds(1, nz - 1)], 1)
    total = b1[z].astype(F32)
    for d in range(1, nz):
        total = total + b1r[d].astype(F32)
    total = total.astype(BF)
    for q in range(ny):
        b2[q] = total[:, q * LANE:(q + 1) * LANE]
    for d in range(1, ny):
        send(b2.at[(y + d) % ny], b2r.at[d], 3, ypeer(d))
    landed(f2r.at[pl.ds(1, nz - 1)], 2)
    total = f2[z].astype(F32)
    for d in range(1, nz):
        total = total + f2r[d].astype(F32)
    low[z, 0] = total.astype(BF)
    landed(b2r.at[pl.ds(1, ny - 1)], 3)
    total = b2[y].astype(F32)
    for d in range(1, ny):
        total = total + b2r[d].astype(F32)
    low[z, 1] = total.astype(BF)
    for d in range(1, nz):
        send(low.at[z], low.at[z], 4, zpeer(d))
    landed(low.at[pl.ds(0, nz - 1)], 4)

    send4[:, 0] = nn(pick[...], low[:, 0].reshape(tok, LANE)).astype(BF).reshape(ndp, PAD, LANE)
    send4[:, 1] = nn(wpick[...], low[:, 1].reshape(tok, LANE)).astype(BF).reshape(ndp, PAD, LANE)
    recv4[0] = send4[0]
    for d in range(1, ndp):
        send(send4.at[d], recv4.at[d], 5, dpeer(d))
    landed(recv4.at[pl.ds(1, ndp - 1)], 5)

    mine = pl.ds(pl.multiple_of(y * LANE, LANE), LANE)
    for p in range(2):
        full[p, :, mine] = nn(pack, recv4[:, p].reshape(slots, LANE)).astype(BF)
    half = ny // 2

    def ring(way, step, p):
        sign = 1 if way == 0 else -1
        at = full.at[p, :, pl.ds(pl.multiple_of(((y - sign * (step - 1) + ny) % ny) * LANE, LANE), LANE)]
        return pltpu.make_async_remote_copy(
            src_ref=at, dst_ref=at,
            send_sem=ysend.at[way, step - 1, p], recv_sem=yrcv.at[way, step - 1, p],
            device_id=ypeer(sign), device_id_type=MESH,
        )

    started = []
    waited = set()

    def ring_wait(way, step, p):
        if (way, step, p) not in waited:
            waited.add((way, step, p))
            ring(way, step, p).wait_recv()

    for step in range(1, half + 1):
        for p in range(2):
            for way in range(2):
                if step == half and way != p:
                    continue
                if step > 1:
                    ring_wait(way, step - 1, p)
                ring(way, step, p).start()
                started.append((way, step, p))
    for p in range(2):
        for way, step, q in started:
            if q == p:
                ring_wait(way, step, q)

    gate = nn(full[0], w_gate[...])
    lift = nn(full[0], w_up[...])
    sigma = jax.nn.sigmoid(gate)
    active = gate * sigma
    hidden = (active * lift).astype(BF)
    own[0] = nn(hidden, w_down[...])

    def lane(q):
        return pl.ds(pl.multiple_of(((q + ny) % ny) * LANE, LANE), LANE)

    def pass_on(way, step, p):
        sign = 1 if way == 0 else -1
        return pltpu.make_async_remote_copy(
            src_ref=ystage.at[way, step - 1, p], dst_ref=yrecv.at[way, step - 1, p],
            send_sem=psend.at[way, step - 1, p], recv_sem=prcv.at[way, step - 1, p],
            device_id=ypeer(sign), device_id_type=MESH,
        )

    def pass_step(step, p):
        for way in range(2):
            sign = 1 if way == 0 else -1
            if step == 1 and way != p:
                continue
            value = own[p, :, lane(y + sign * (half + 1 - step))]
            if step > 2 or (step == 2 and way == p):
                pass_on(way, step - 1, p).wait_recv()
                value = value + yrecv[way, step - 2, p].astype(F32)
            ystage[way, step - 1, p] = value.astype(BF)
            pass_on(way, step, p).start()

    def pass_end(p):
        value = own[p, :, lane(y)]
        for way in range(2):
            if half == 1 and way != p:
                continue
            pass_on(way, half, p).wait_recv()
            value = value + yrecv[way, half - 1, p].astype(F32)
        return value.astype(BF)

    pass_step(1, 0)
    hidden_grad = nt(full[1], w_down[...])
    gate_grad = (hidden_grad * lift * (sigma * (1.0 + gate * (1.0 - sigma)))).astype(BF)
    lift_grad = (hidden_grad * active).astype(BF)
    own[1] = nt(gate_grad, w_gate[...]) + nt(lift_grad, w_up[...])
    pass_step(1, 1)
    work = [
        lambda: gate_out.__setitem__(..., tn(full[0], gate_grad).astype(BF)),
        lambda: lift_out.__setitem__(..., tn(full[0], lift_grad).astype(BF)),
        lambda: dexp_out.__setitem__(..., tn(hidden, full[1]).astype(BF)),
    ]
    for step in range(2, half + 1):
        pass_step(step, 0)
        pass_step(step, 1)
        if work:
            work.pop(0)()
    while work:
        work.pop(0)()

    for p in range(2):
        back[:, p] = nn(unpack, pass_end(p)).astype(BF).reshape(ndp, PAD, LANE)
    backr[0] = back[0]
    for d in range(1, ndp):
        send(back.at[d], backr.at[d], 6, dpeer(-d))
    landed(backr.at[pl.ds(1, ndp - 1)], 6)

    z1[:, 0] = tn(wpick[...], backr[:, 0].reshape(slots, LANE)).astype(BF).reshape(nz, rows, LANE)
    z1[:, 1] = tn(pick[...], backr[:, 1].reshape(slots, LANE)).astype(BF).reshape(nz, rows, LANE)
    for d in range(1, nz):
        send(z1.at[(z + d) % nz], z1r.at[d], 7, zpeer(d))
    padc[...] = jnp.zeros_like(padc)
    padt[...] = jnp.zeros_like(padt)
    padc[:, :wide] = cot[...]
    padt[:, :wide] = tokens[...]
    landed(z1r.at[pl.ds(1, nz - 1)], 7)
    total = z1[z].astype(F32)
    for d in range(1, nz):
        total = total + z1r[d].astype(F32)
    cf1[z] = total[0].astype(BF)
    cb1[:, mine] = total[1].astype(BF)
    for d in range(1, nz):
        send(cf1.at[z], cf1.at[z], 8, zpeer(d))
    for d in range(1, ny):
        send(cb1.at[:, mine], cb1.at[:, mine], 9, ypeer(d))
    landed(cf1.at[pl.ds(0, nz - 1)], 8)
    cf[:, :, mine] = cf1[...]
    for d in range(1, ny):
        send(cf1, cf.at[:, :, mine], 10, ypeer(d))
    landed(cb1.at[:, pl.ds(0, (ny - 1) * LANE)], 9)
    cb[z] = cb1[...]
    for d in range(1, nz):
        send(cb1, cb.at[z], 11, zpeer(d))

    landed(cf.at[:, :, pl.ds(0, (ny - 1) * LANE)], 10)
    whole = cf[...].reshape(tok, latent)
    up_part = tn(whole, padc[...]).astype(BF)
    layer_out[...] = nn(whole, up[...]).astype(BF)
    landed(cb.at[pl.ds(0, nz - 1)], 11)
    whole = cb[...].reshape(tok, latent)
    down_part = tn(whole, padt[...]).astype(BF)
    token_grad[...] = nt(whole, down[...]).astype(BF)
    for q in range(ndp):
        g1[q % 2, q // 2, 0] = up_part[q * part:(q + 1) * part]
        g1[q % 2, q // 2, 1] = down_part[q * part:(q + 1) * part]
    send(g1.at[1 - core], g1r, 12, sibling)
    landed(g1r, 12)
    g2[...] = (g1[core].astype(F32) + g1r[...].astype(F32)).astype(BF)
    for d in range(1, nx):
        send(g2.at[(xi + d) % nx], g2r.at[d], 13, xpeer(d))
    landed(g2r.at[pl.ds(1, nx - 1)], 13)
    total = g2[xi].astype(F32)
    for d in range(1, nx):
        total = total + g2r[d].astype(F32)
    up_grad[...] = total[0, :, :wide]
    down_grad[...] = total[1, :, :wide]

    for ref, phase in pending:
        pltpu.make_async_remote_copy(
            src_ref=ref, dst_ref=ref, send_sem=ssem.at[phase], recv_sem=rsem.at[phase],
            device_id=sibling, device_id_type=MESH,
        ).wait_send()
    for way, step, p in started:
        ring(way, step, p).wait_send()
    for p in range(2):
        for step in range(1, half + 1):
            for way in range(2):
                if not (step == 1 and way != p):
                    pass_on(way, step, p).wait_send()


def make(mesh, ny):
    ndp, nex = mesh.shape["dp"], mesh.shape["expert"]
    nz = nex // ny
    nx = ndp // 2
    half = ny // 2

    def local(tokens, routes, scores, down, up, w_gate, w_up, w_down, cot):
        tok, wide = tokens.shape
        latent, hid = w_gate.shape
        rows, part = tok // nz, latent // ndp
        packed = ndp * CAP
        shape = jax.ShapeDtypeStruct

        def vm(*dims, kind=BF):
            return pltpu.VMEM(dims, kind)

        outs = pl.pallas_call(
            functools.partial(kernel, ndp, nz, ny),
            out_shape=(
                shape((tok, wide), BF),
                shape((tok, wide), BF),
                shape((part, wide), F32),
                shape((part, wide), F32),
                shape((latent, hid), BF),
                shape((latent, hid), BF),
                shape((hid, latent), BF),
            ),
            in_specs=[pl.BlockSpec(memory_space=pltpu.VMEM)] * 9,
            out_specs=[pl.BlockSpec(memory_space=pltpu.VMEM)] * 7,
            scratch_shapes=[
                vm(ny, tok, LANE), vm(ny, tok, LANE), vm(nz, rows, LANE), vm(nz, rows, LANE),
                vm(nz, rows, latent), vm(nz, rows, latent), vm(ny, rows, LANE), vm(ny, rows, LANE),
                vm(nz, 2, rows, LANE),
                vm(ndp * PAD, tok), vm(ndp * PAD, tok),
                vm(ndp, 2, PAD, LANE), vm(ndp, 2, PAD, LANE),
                vm(2, packed, latent),
                vm(2, half, 2, packed, LANE), vm(2, half, 2, packed, LANE),
                vm(2, packed, latent, kind=F32),
                vm(ndp, 2, PAD, LANE), vm(ndp, 2, PAD, LANE),
                vm(nz, 2, rows, LANE), vm(nz, 2, rows, LANE),
                vm(nz, rows, LANE), vm(rows, latent), vm(nz, rows, latent), vm(nz, rows, latent),
                vm(tok, LANE), vm(tok, LANE),
                vm(2, nx, 2, part, LANE), vm(nx, 2, part, LANE), vm(nx, 2, part, LANE), vm(nx, 2, part, LANE),
                pltpu.SemaphoreType.DMA((14,)), pltpu.SemaphoreType.DMA((14,)),
                pltpu.SemaphoreType.DMA((2, half, 2)), pltpu.SemaphoreType.DMA((2, half, 2)),
                pltpu.SemaphoreType.DMA((2, half, 2)), pltpu.SemaphoreType.DMA((2, half, 2)),
            ],
            compiler_params=pltpu.CompilerParams(
                collective_id=0, has_side_effects=True, vmem_limit_bytes=56 * 1024 * 1024,
            ),
        )(tokens, routes.T, scores.T, down, up, w_gate, w_up, w_down, cot)
        layer_out, token_grad, down_grad, up_grad, gate_out, lift_out, dexp_out = outs
        return layer_out, token_grad, down_grad.T, up_grad, gate_out, lift_out, dexp_out

    return jax.shard_map(
        local, mesh=mesh,
        in_specs=(
            P("dp", "expert"), P("dp", None), P("dp", None), P("expert", None), P(None, "expert"),
            P(None, ("dp", "expert")), P(None, ("dp", "expert")), P(("dp", "expert"), None), P("dp", "expert"),
        ),
        out_specs=(
            P("dp", "expert"), P("dp", "expert"), P("expert", "dp"), P("dp", "expert"),
            P(None, ("dp", "expert")), P(None, ("dp", "expert")), P(("dp", "expert"), None),
        ),
        check_vma=False,
    )


def solution(mesh):
    return make(mesh, NY)
```

time: 811 us -> 128 us (0.16)
  blocking collectives: 476 us -> 0 us
  waiting for transfers between devices: 222 us -> 0 us
  Pallas kernels: 0 us -> 115 us
  starting transfers between devices: 73 us -> 0 us
  between operations: 14.4 us -> 0.67 us
  matrix products: 10.4 us -> 0 us
    psum x2 -> x0, blocking collectives: 476 us -> none  [column_total(): whole = lax.psum(term_fn(0, tok_row), 'expert')]
    pallas_call x0 -> x1, Pallas kernels: none -> 115 us  [local(): pl.pallas_call(functools.partial(kernel, ndp, nz, ny), out_shape=(shape((...]
    unnamed x3 -> x0, waiting for transfers between devices: 98.4 us -> none
    all_to_all x4 -> x0, starting transfers between devices: 72.9 us -> none  [the longest x2 65.9 us: to_experts(): lax.all_to_all(outgoing, 'dp', split_axis=0, concat_axis=0, tiled=True)]
    reduce_scatter x1 -> x0, waiting for transfers between devices: 63 us -> none  [local(): lax.psum_scatter(up_part.astype(jnp.bfloat16), 'dp', scatter_dimension=0,...]
    all_to_all x4 -> x0, waiting for transfers between devices: 60.3 us -> none  [the longest x2 30.9 us: to_experts(): lax.all_to_all(outgoing, 'dp', split_axis=0, concat_axis=0, tiled=True)]
    dot_general x19 -> x0, matrix products: 10.4 us -> none  [the longest x1 1.15 us: local(): jnp.dot(slot_rows.T, gate_grad, preferred_element_type=jnp.float32)]
  transfers between devices with their start and end apart: 6 -> 0, of which waited for: 6 -> 0; matrix products, arithmetic and copies ran while one was open for 1% -> 0% of each run, Pallas kernels for 0% -> 0%
where the time goes in v1:
time: 128 us; the launch traced here: 127 us
  Pallas kernels  115 us (90%)
  local copies, waits for them, and re-layouts  11.5 us (9%)
    pallas_call x1, Pallas kernels, local(): pl.pallas_call(functools.partial(kernel, ndp, nz, ny), out_shape=(shape((...  115 us
    unnamed x22, local copies, waits for them, and re-layouts  11.5 us

profile of v1, /device:TPU:1, one launch (start us, length us, event | category | flops | bytes accessed | tf_op | source)
XLA Modules:
  0.0 127.1 jit_solution(6203434627066073667)
XLA Ops:
  0.6 0.0 copy-start.5
  0.6 1.5 %copy.16.tokens = bf16[128,112]{1,0:T(8,128)(2,1)} copy(bf16[128,112]{0,1:T(8,128)(2,1)} %param.9) | data formatting | bytes 57344 | tf_op args[0]
  2.1 0.0 copy-done.5
  2.1 0.7 copy.18.cot
  2.8 1.8 %copy.17.up = bf16[1024,112]{1,0:T(8,128)(2,1)} copy(bf16[1024,112]{0,1:T(8,128)(2,1)} %param.13) | data formatting | bytes 458752 | tf_op args[4]
  4.6 114.9 %shard_map.144 = (bf16[128,112]{1,0:T(8,128)(2,1)}, bf16[128,112]{1,0:T(8,128)(2,1)}, f32[64,112]{1,0:T(8,128)}, f32[64,112]{1,0:T(8,128)}, bf16[1024,256]{1,0:T...) custom-call(bf16[128,112]{1,0:T(8,128)(2,1)} %copy.16.tokens, s32[4,128]{1,0:T(4,128)} %bitcast.4, ...), custom_call_target="tpu_custom_call" | custom-call | tf_op jit(solution)/shard_map/pallas_call | solution.py:348
  119.5 0.0 copy-start.4
  119.5 1.5 %copy.19 = bf16[128,112]{0,1:T(8,128)(2,1)} copy(bf16[128,112]{1,0:T(8,128)(2,1)} %get-tuple-element.21) | data formatting | bytes 57344
  121.0 0.0 copy-done.4
  121.0 0.0 copy-start.3
  121.0 0.7 copy.20
  121.7 0.0 copy-done.3
  121.7 0.0 copy-start.2
  121.7 0.6 copy.26
  122.4 0.2 copy-done.2
  122.5 0.6 copy.27
  123.1 0.0 copy-start.1
  123.1 1.9 %copy.28 = bf16[1024,256]{1,0:T(8,128)(2,1)} copy(bf16[1024,256]{1,0:T(8,128)(2,1)} %get-tuple-element.39) | data formatting | bytes 1048576
  125.1 0.0 copy-done.1
  125.1 0.0 copy-start
  125.1 0.8 copy.29
  125.9 0.4 copy-done
  126.3 0.8 copy.30
Async XLA Ops:
  0.6 1.5 %copy-start.5 = (bf16[128,112]{0,1:T(8,128)(2,1)S(1)}, bf16[128,112]{0,1:T(8,128)(2,1)}, u32[]{:S(2)}) copy-start(bf16[128,112]{0,1:T(8,128)(2,1)} %param.17) | copy-start | bytes 86020
  119.5 1.5 %copy-start.4 = (bf16[128,112]{1,0:T(8,128)(2,1)S(1)}, bf16[128,112]{1,0:T(8,128)(2,1)}, u32[]{:S(2)}) copy-start(bf16[128,112]{1,0:T(8,128)(2,1)} %get-tuple-element.22) | copy-start | bytes 86020
  121.0 0.8 copy-start.3
  121.7 0.8 copy-start.2
  123.1 1.9 %copy-start.1 = (bf16[1024,256]{1,0:T(8,128)(2,1)S(1)}, bf16[1024,256]{1,0:T(8,128)(2,1)}, u32[]{:S(2)}) copy-start(bf16[1024,256]{1,0:T(8,128)(2,1)} %get-tuple-element.40) | copy-start | bytes 1572868
  125.1 1.2 copy-start

commit v2 on v1

v2 whole, which is shorter than its diff:
```python
import functools

import jax
import jax.numpy as jnp
from jax import lax
from jax.experimental import pallas as pl
from jax.experimental.pallas import tpu as pltpu
from jax.sharding import PartitionSpec as P

MESH = pl.DeviceIdType.MESH
BF = jnp.bfloat16
F32 = jnp.float32
NY = 8
CAP = 12
PAD = 16
LANE = 128
CUT = 2


def nn(a, b):
    return jnp.dot(a, b, preferred_element_type=F32)


def nt(a, b):
    return lax.dot_general(a, b, (((1,), (1,)), ((), ())), preferred_element_type=F32)


def tn(a, b):
    return lax.dot_general(a, b, (((0,), (0,)), ((), ())), preferred_element_type=F32)


def kernel(
    ndp, nz, ny,
    hbm_tokens, routes, scores, hbm_proj, hbm_back, hbm_gate, hbm_up, hbm_down, hbm_cot,
    layer_out, token_grad, down_grad, up_grad, hbm_gate_out, hbm_lift_out, hbm_dexp_out,
    tokens, down, up, cot, w_gate, w_up, w_down, gate_out, lift_out, dexp_out, isem, osem,
    f1, f1r, f2, f2r, b1, b1r, b2, b2r, low,
    pick, send4, recv4, full, ystage, yrecv, own, back, backr,
    z1, z1r, cf1, cb1, cf, cb, padded, g1, g1r, g2, g2r,
    ssem, rsem, ysend, yrcv, psend, prcv,
):
    dp = lax.axis_index("dp")
    ex = lax.axis_index("expert")
    z, y = ex // ny, ex % ny
    xi, core = dp // 2, dp % 2
    nx = ndp // 2
    wide, tok = tokens.shape
    latent = down.shape[1]
    rows = tok // nz
    slots = ndp * PAD
    packed = ndp * CAP

    def ypeer(d):
        return (dp, z * ny + (y + d + ny) % ny)

    def zpeer(d):
        return (dp, ((z + d + nz) % nz) * ny + y)

    def dpeer(d):
        return ((dp + d + ndp) % ndp, ex)

    def xpeer(d):
        return (((xi + d + nx) % nx) * 2 + core, ex)

    def far(count):
        return sorted(range(1, count), key=lambda d: -min(d, count - d))

    sibling = (xi * 2 + 1 - core, ex)

    pending = []

    def finish():
        for wait in pending:
            wait()

    fetch = [
        pltpu.make_async_copy(src, dst, isem.at[n])
        for n, (src, dst) in enumerate((
            (hbm_tokens, tokens), (hbm_proj, down), (hbm_cot, cot), (hbm_back, up),
            (hbm_gate, w_gate), (hbm_up, w_up), (hbm_down, w_down),
        ))
    ]
    for copy in fetch:
        copy.start()

    def send(src, dst, phase, device):
        pltpu.make_async_remote_copy(
            src_ref=src, dst_ref=dst, send_sem=ssem.at[phase], recv_sem=rsem.at[phase],
            device_id=device, device_id_type=MESH,
        ).start()

    def landed(ref, phase):
        whole = pltpu.make_async_remote_copy(
            src_ref=ref, dst_ref=ref, send_sem=ssem.at[phase], recv_sem=rsem.at[phase],
            device_id=sibling, device_id_type=MESH,
        )
        whole.wait_recv()
        pending.append(whole.wait_send)

    barrier = pltpu.get_barrier_semaphore()
    for d in range(1, ny):
        pl.semaphore_signal(barrier, inc=1, device_id=ypeer(d), device_id_type=MESH)
    for d in range(1, nz):
        pl.semaphore_signal(barrier, inc=1, device_id=zpeer(d), device_id_type=MESH)
    for d in range(1, ndp):
        pl.semaphore_signal(barrier, inc=1, device_id=dpeer(d), device_id_type=MESH)

    fetch[0].wait()
    fetch[1].wait()
    part = tn(tokens[...], down[...]).astype(BF)
    for q in range(ny):
        f1[q] = part[:, q * LANE:(q + 1) * LANE]
    pl.semaphore_wait(barrier, ny + nz + ndp - 3)
    for d in far(ny):
        send(f1.at[(y + d) % ny], f1r.at[d], 0, ypeer(d))
    fetch[2].wait()
    fetch[3].wait()
    part = tn(cot[...], up[...]).astype(BF)
    for q in range(nz):
        b1[q] = part[q * rows:(q + 1) * rows]
    for d in far(nz):
        send(b1.at[(z + d) % nz], b1r.at[d], 1, zpeer(d))

    r = routes[...]
    s = scores[...].astype(F32)
    share = s / jnp.sum(s, axis=0, keepdims=True)
    target = lax.broadcasted_iota(jnp.int32, (ndp, tok), 0) + dp
    target = jnp.where(target >= ndp, target - ndp, target) * nz + z
    member = jnp.zeros((ndp, tok), F32)
    weight = jnp.zeros((ndp, tok), F32)
    for k in range(r.shape[0]):
        hit = r[k:k + 1] == target
        member = member + jnp.where(hit, 1.0, 0.0)
        weight = weight + jnp.where(hit, share[k:k + 1], 0.0)
    ahead = lax.broadcasted_iota(jnp.int32, (tok, tok), 0) < lax.broadcasted_iota(jnp.int32, (tok, tok), 1)
    place = nn(member.astype(BF), jnp.where(ahead, 1.0, 0.0).astype(BF))
    place = jnp.where(member > 0.5, place, -1.0).astype(jnp.int32)
    spot = lax.broadcasted_iota(jnp.int32, (PAD, tok), 0)
    for d in range(ndp):
        hit = place[d:d + 1] == spot
        pick[0, d * PAD:(d + 1) * PAD] = jnp.where(hit, 1.0, 0.0).astype(BF)
        pick[1, d * PAD:(d + 1) * PAD] = jnp.where(hit, weight[d:d + 1], 0.0).astype(BF)
    row = lax.broadcasted_iota(jnp.int32, (packed, slots), 0)
    col = lax.broadcasted_iota(jnp.int32, (packed, slots), 1)
    pack = jnp.where((col - row == (col >> 4) * (PAD - CAP)) & ((col & (PAD - 1)) < CAP), 1.0, 0.0).astype(BF)
    row = lax.broadcasted_iota(jnp.int32, (slots, packed), 0)
    col = lax.broadcasted_iota(jnp.int32, (slots, packed), 1)
    unpack = jnp.where((row - col == (row >> 4) * (PAD - CAP)) & ((row & (PAD - 1)) < CAP), 1.0, 0.0).astype(BF)
    padded[...] = jnp.zeros_like(padded)
    padded[0, :, :wide] = cot[...].T
    padded[1, :, :wide] = tokens[...].T

    def gathered(first, others, count):
        total = first.astype(F32)
        for d in range(1, count):
            total = total + others[d].astype(F32)
        return total

    landed(f1r.at[pl.ds(1, ny - 1)], 0)
    total = gathered(f1[y], f1r, ny).astype(BF)
    for q in range(nz):
        f2[q] = total[q * rows:(q + 1) * rows]
    for d in far(nz):
        send(f2.at[(z + d) % nz], f2r.at[d], 2, zpeer(d))
    landed(b1r.at[pl.ds(1, nz - 1)], 1)
    total = gathered(b1[z], b1r, nz).astype(BF)
    for q in range(ny):
        b2[q] = total[:, q * LANE:(q + 1) * LANE]
    for d in far(ny):
        send(b2.at[(y + d) % ny], b2r.at[d], 3, ypeer(d))
    landed(f2r.at[pl.ds(1, nz - 1)], 2)
    low[0, z] = gathered(f2[z], f2r, nz).astype(BF)
    for d in far(nz):
        send(low.at[0, z], low.at[0, z], 4, zpeer(d))
    landed(b2r.at[pl.ds(1, ny - 1)], 3)
    low[1, z] = gathered(b2[y], b2r, ny).astype(BF)
    for d in far(nz):
        send(low.at[1, z], low.at[1, z], 5, zpeer(d))

    for p in range(2):
        landed(low.at[p, pl.ds(0, nz - 1)], 4 + p)
        value = nn(pick[p], low[p].reshape(tok, LANE))
        send4[p] = value.astype(BF).reshape(ndp, PAD, LANE)
        for d in far(ndp):
            send(send4.at[p, d], recv4.at[p, d], 6 + p, dpeer(d))
        recv4[p, 0] = send4[p, 0]

    mine = pl.ds(pl.multiple_of(y * LANE, LANE), LANE)
    half = ny // 2
    piece = packed // CUT

    def lane(q):
        return pl.ds(pl.multiple_of(((q + ny) % ny) * LANE, LANE), LANE)

    def skips(way, k):
        return way != k % 2

    def ring(way, step, k):
        sign = 1 if way == 0 else -1
        at = full.at[k // CUT, pl.ds(k % CUT * piece, piece), lane(y - sign * (step - 1))]
        return pltpu.make_async_remote_copy(
            src_ref=at, dst_ref=at,
            send_sem=ysend.at[way, step - 1, k], recv_sem=yrcv.at[way, step - 1, k],
            device_id=ypeer(sign), device_id_type=MESH,
        )

    waited = set()

    def ring_wait(way, step, k):
        if (way, step, k) not in waited:
            waited.add((way, step, k))
            ring(way, step, k).wait_recv()

    def ring_step(step, p):
        for k in range(p * CUT, (p + 1) * CUT):
            for way in range(2):
                if step == half and skips(way, k):
                    continue
                if step > 1:
                    ring_wait(way, step - 1, k)
                ring(way, step, k).start()
                pending.append(ring(way, step, k).wait_send)

    def ring_end(p):
        for step in range(1, half + 1):
            for k in range(p * CUT, (p + 1) * CUT):
                for way in range(2):
                    if not (step == half and skips(way, k)):
                        ring_wait(way, step, k)

    for p in range(2):
        landed(recv4.at[p, pl.ds(1, ndp - 1)], 6 + p)
        full[p, :, mine] = nn(pack, recv4[p].reshape(slots, LANE)).astype(BF)
        ring_step(1, p)
    for step in range(2, half + 1):
        for p in range(2):
            ring_step(step, p)
    ring_end(0)

    for copy in fetch[4:]:
        copy.wait()
    gate = nn(full[0], w_gate[...])
    lift = nn(full[0], w_up[...])
    sigma = jax.nn.sigmoid(gate)
    active = gate * sigma
    hidden = (active * lift).astype(BF)
    own[0] = nn(hidden, w_down[...])

    def pass_on(way, step, k):
        sign = 1 if way == 0 else -1
        return pltpu.make_async_remote_copy(
            src_ref=ystage.at[way, step - 1, k], dst_ref=yrecv.at[way, step - 1, k],
            send_sem=psend.at[way, step - 1, k], recv_sem=prcv.at[way, step - 1, k],
            device_id=ypeer(sign), device_id_type=MESH,
        )

    def pass_step(step, p):
        for k in range(p * CUT, (p + 1) * CUT):
            for way in range(2):
                sign = 1 if way == 0 else -1
                if step == 1 and skips(way, k):
                    continue
                value = own[p, pl.ds(k % CUT * piece, piece), lane(y + sign * (half + 1 - step))]
                if step > 2 or (step == 2 and not skips(way, k)):
                    pass_on(way, step - 1, k).wait_recv()
                    value = value + yrecv[way, step - 2, k].astype(F32)
                ystage[way, step - 1, k] = value.astype(BF)
                pass_on(way, step, k).start()
                pending.append(pass_on(way, step, k).wait_send)

    def pass_end(p):
        parts = []
        for k in range(p * CUT, (p + 1) * CUT):
            value = own[p, pl.ds(k % CUT * piece, piece), lane(y)]
            for way in range(2):
                if half == 1 and skips(way, k):
                    continue
                pass_on(way, half, k).wait_recv()
                value = value + yrecv[way, half - 1, k].astype(F32)
            parts.append(value.astype(BF))
        return jnp.concatenate(parts, axis=0)

    pass_step(1, 0)
    ring_end(1)
    hidden_grad = nt(full[1], w_down[...])
    gate_grad = (hidden_grad * lift * (sigma * (1.0 + gate * (1.0 - sigma)))).astype(BF)
    lift_grad = (hidden_grad * active).astype(BF)
    own[1] = nt(gate_grad, w_gate[...]) + nt(lift_grad, w_up[...])
    pass_step(1, 1)
    work = [
        (gate_out, hbm_gate_out, lambda: tn(full[0], gate_grad)),
        (lift_out, hbm_lift_out, lambda: tn(full[0], lift_grad)),
        (dexp_out, hbm_dexp_out, lambda: tn(hidden, full[1])),
    ]

    def do_work():
        held, out, product = work.pop(0)
        held[...] = product().astype(BF)
        copy = pltpu.make_async_copy(held, out, osem.at[len(work)])
        copy.start()
        pending.append(copy.wait)

    for step in range(2, half + 1):
        pass_step(step, 0)
        pass_step(step, 1)
        if work:
            do_work()
    while work:
        do_work()

    for p in range(2):
        back[p] = nn(unpack, pass_end(p)).astype(BF).reshape(ndp, PAD, LANE)
        for d in far(ndp):
            send(back.at[p, d], backr.at[p, d], 8 + p, dpeer(-d))
        backr[p, 0] = back[p, 0]

    for p in range(2):
        landed(backr.at[p, pl.ds(1, ndp - 1)], 8 + p)
        value = tn(pick[1 - p], backr[p].reshape(slots, LANE))
        z1[p] = value.astype(BF).reshape(nz, rows, LANE)
        for d in far(nz):
            send(z1.at[p, (z + d) % nz], z1r.at[p, d], 10 + p, zpeer(d))
    landed(z1r.at[0, pl.ds(1, nz - 1)], 10)
    cf1[z] = gathered(z1[0, z], z1r.at[0], nz).astype(BF)
    for d in far(nz):
        send(cf1.at[z], cf1.at[z], 12, zpeer(d))
    landed(z1r.at[1, pl.ds(1, nz - 1)], 11)
    cb1[:, mine] = gathered(z1[1, z], z1r.at[1], nz).astype(BF)
    for d in far(ny):
        send(cb1.at[:, mine], cb1.at[:, mine], 13, ypeer(d))
    landed(cf1.at[pl.ds(0, nz - 1)], 12)
    for d in far(ny):
        send(cf1, cf.at[:, :, mine], 14, ypeer(d))
    cf[:, :, mine] = cf1[...]
    landed(cb1.at[:, pl.ds(0, (ny - 1) * LANE)], 13)
    for d in far(nz):
        send(cb1, cb.at[z], 15, zpeer(d))
    cb[z] = cb1[...]

    share_rows = latent // ndp
    for p, (ref, wait) in enumerate((
        (cf, cf.at[:, :, pl.ds(0, (ny - 1) * LANE)]), (cb, cb.at[pl.ds(0, nz - 1)]),
    )):
        landed(wait, 14 + p)
        value = tn(ref[...].reshape(tok, latent), padded[p]).astype(BF)
        for q in range(ndp):
            g1[p, q % 2, q // 2] = value[q * share_rows:(q + 1) * share_rows]
        send(g1.at[p, 1 - core], g1r.at[p], 16 + p, sibling)
    for p in range(2):
        landed(g1r.at[p], 16 + p)
        g2[p] = (g1[p, core].astype(F32) + g1r[p].astype(F32)).astype(BF)
        for d in far(nx):
            send(g2.at[p, (xi + d) % nx], g2r.at[p, d], 18 + p, xpeer(d))
    layer_out[...] = nt(up[...], cf[...].reshape(tok, latent)).astype(BF)
    token_grad[...] = nt(down[...], cb[...].reshape(tok, latent)).astype(BF)
    for p, out in enumerate((up_grad, down_grad)):
        landed(g2r.at[p, pl.ds(1, nx - 1)], 18 + p)
        out[...] = gathered(g2[p, xi], g2r.at[p], nx)[:, :wide]
    finish()


def hand_over(*refs):
    count = (len(refs) - 2) // 3
    given, outs, held = refs[:count], refs[count:2 * count], refs[2 * count:3 * count]
    arrived, left = refs[3 * count:]
    ins = [pltpu.make_async_copy(given[n], held[n], arrived.at[n]) for n in range(count)]
    out = [pltpu.make_async_copy(held[n], outs[n], left.at[n]) for n in range(count)]
    for copy in ins:
        copy.start()
    for n in range(count):
        ins[n].wait()
        out[n].start()
    for copy in out:
        copy.wait()


def make(mesh, ny):
    ndp, nex = mesh.shape["dp"], mesh.shape["expert"]
    nz = nex // ny
    nx = ndp // 2
    half = ny // 2

    def local(tokens, routes, scores, down, up, w_gate, w_up, w_down, cot):
        tokens, cot, up = tokens.T, cot.T, up.T
        wide, tok = tokens.shape
        latent, hid = w_gate.shape
        rows, part = tok // nz, latent // ndp
        packed = ndp * CAP
        shape = jax.ShapeDtypeStruct
        inside = pl.BlockSpec(memory_space=pltpu.VMEM)
        outside = pl.BlockSpec(memory_space=pl.ANY)

        def vm(*dims, kind=BF):
            return pltpu.VMEM(dims, kind)

        outs = pl.pallas_call(
            functools.partial(kernel, ndp, nz, ny),
            out_shape=(
                shape((wide, tok), BF),
                shape((wide, tok), BF),
                shape((part, wide), F32),
                shape((part, wide), F32),
                shape((latent, hid), BF),
                shape((latent, hid), BF),
                shape((hid, latent), BF),
            ),
            in_specs=[outside] + [inside] * 2 + [outside] * 6,
            out_specs=[inside] * 4 + [outside] * 3,
            scratch_shapes=[
                vm(wide, tok), vm(wide, latent), vm(wide, latent), vm(wide, tok),
                vm(latent, hid), vm(latent, hid), vm(hid, latent),
                vm(latent, hid), vm(latent, hid), vm(hid, latent),
                pltpu.SemaphoreType.DMA((7,)), pltpu.SemaphoreType.DMA((3,)),
                vm(ny, tok, LANE), vm(ny, tok, LANE), vm(nz, rows, LANE), vm(nz, rows, LANE),
                vm(nz, rows, latent), vm(nz, rows, latent), vm(ny, rows, LANE), vm(ny, rows, LANE),
                vm(2, nz, rows, LANE),
                vm(2, ndp * PAD, tok),
                vm(2, ndp, PAD, LANE), vm(2, ndp, PAD, LANE),
                vm(2, packed, latent),
                vm(2, half, 2 * CUT, packed // CUT, LANE), vm(2, half, 2 * CUT, packed // CUT, LANE),
                vm(2, packed, latent, kind=F32),
                vm(2, ndp, PAD, LANE), vm(2, ndp, PAD, LANE),
                vm(2, nz, rows, LANE), vm(2, nz, rows, LANE),
                vm(nz, rows, LANE), vm(rows, latent), vm(nz, rows, latent), vm(nz, rows, latent),
                vm(2, tok, LANE),
                vm(2, 2, nx, part, LANE), vm(2, nx, part, LANE), vm(2, nx, part, LANE), vm(2, nx, part, LANE),
                pltpu.SemaphoreType.DMA((20,)), pltpu.SemaphoreType.DMA((20,)),
                pltpu.SemaphoreType.DMA((2, half, 2 * CUT)), pltpu.SemaphoreType.DMA((2, half, 2 * CUT)),
                pltpu.SemaphoreType.DMA((2, half, 2 * CUT)), pltpu.SemaphoreType.DMA((2, half, 2 * CUT)),
            ],
            compiler_params=pltpu.CompilerParams(
                collective_id=0, has_side_effects=True, vmem_limit_bytes=56 * 1024 * 1024,
            ),
        )(tokens, routes.T, scores.T, down, up, w_gate, w_up, w_down, cot)
        layer_out, token_grad, down_grad, up_grad, gate_out, lift_out, dexp_out = pl.pallas_call(
            hand_over,
            out_shape=[shape(out.shape, out.dtype) for out in outs],
            in_specs=[outside] * len(outs),
            out_specs=[outside] * len(outs),
            scratch_shapes=[vm(*out.shape, kind=out.dtype) for out in outs] + [
                pltpu.SemaphoreType.DMA((len(outs),)), pltpu.SemaphoreType.DMA((len(outs),)),
            ],
            compiler_params=pltpu.CompilerParams(vmem_limit_bytes=58 * 1024 * 1024),
        )(*outs)
        return layer_out.T, token_grad.T, down_grad.T, up_grad, gate_out, lift_out, dexp_out

    return jax.shard_map(
        local, mesh=mesh,
        in_specs=(
            P("dp", "expert"), P("dp", None), P("dp", None), P("expert", None), P(None, "expert"),
            P(None, ("dp", "expert")), P(None, ("dp", "expert")), P(("dp", "expert"), None), P("dp", "expert"),
        ),
        out_specs=(
            P("dp", "expert"), P("dp", "expert"), P("expert", "dp"), P("dp", "expert"),
            P(None, ("dp", "expert")), P(None, ("dp", "expert")), P(("dp", "expert"), None),
        ),
        check_vma=False,
    )


def solution(mesh):
    return make(mesh, NY)
```

time: 128 us -> 109 us (0.85)
  local copies, waits for them, and re-layouts: 11.5 us -> 0 us
  Pallas kernels: 115 us -> 108 us
    unnamed x22 -> x0, local copies, waits for them, and re-layouts: 11.5 us -> none
    pallas_call x1, Pallas kernels: 115 us -> 106 us  [local(): pl.pallas_call(functools.partial(kernel, ndp, nz, ny), out_shape=(shape((...]
    pallas_call x0 -> x1, Pallas kernels: none -> 2.38 us  [local(): pl.pallas_call(hand_over, out_shape=[shape(out.shape, out.dtype) for out...]
where the time goes in v2:
time: 109 us
  Pallas kernels  108 us (99%)
    pallas_call x1, Pallas kernels, local(): pl.pallas_call(functools.partial(kernel, ndp, nz, ny), out_shape=(shape((...  106 us
    pallas_call x1, Pallas kernels, local(): pl.pallas_call(hand_over, out_shape=[shape(out.shape, out.dtype) for out...  2.38 us

profile of v2, /device:TPU:1, one launch (start us, length us, event | category | flops | bytes accessed | tf_op | source)
XLA Modules:
  0.0 108.6 jit_solution(4796625073401362502)
XLA Ops:
  0.6 105.6 %shard_map.144 = (bf16[112,128]{1,0:T(8,128)(2,1)}, bf16[112,128]{1,0:T(8,128)(2,1)}, f32[64,112]{1,0:T(8,128)}, f32[64,112]{1,0:T(8,128)}, bf16[1024,256]{1,0:T...) custom-call(bf16[112,128]{1,0:T(8,128)(2,1)} %bitcast.9, s32[4,128]{1,0:T(4,128)} %bitcast.11, ...), custom_call_target="tpu_custom_call" | custom-call | tf_op jit(solution)/shard_map/pallas_call | solution.py:396
  106.2 2.4 %shard_map.145 = (bf16[112,128]{1,0:T(8,128)(2,1)}, bf16[112,128]{1,0:T(8,128)(2,1)}, f32[64,112]{1,0:T(8,128)}, f32[64,112]{1,0:T(8,128)}, bf16[1024,256]{1,0:T...) custom-call(bf16[112,128]{1,0:T(8,128)(2,1)} %get-tuple-element.21.refs_0_, ...), custom_call_target="tpu_custom_call" | custom-call | tf_op jit(solution)/shard_map/pallas_call | solution.py:435

commit v3 on v2

--- a/solution.py
+++ b/solution.py
@@ -14,7 +14,7 @@
 CAP = 12
 PAD = 16
 LANE = 128
-CUT = 2
+CUT = 1
 
 
 def nn(a, b):
@@ -186,56 +186,49 @@
         recv4[p, 0] = send4[p, 0]
 
     mine = pl.ds(pl.multiple_of(y * LANE, LANE), LANE)
-    half = ny // 2
     piece = packed // CUT
 
     def lane(q):
         return pl.ds(pl.multiple_of(((q + ny) % ny) * LANE, LANE), LANE)
 
-    def skips(way, k):
-        return way != k % 2
-
-    def ring(way, step, k):
+    def pieces(p):
+        return [(k, way) for k in range(p * CUT, (p + 1) * CUT) for way in range(2)]
+
+    def hop(way, leg, k):
         sign = 1 if way == 0 else -1
-        at = full.at[k // CUT, pl.ds(k % CUT * piece, piece), lane(y - sign * (step - 1))]
+        source = y if leg < 2 else y - 2 * sign
+        at = full.at[k // CUT, pl.ds(k % CUT * piece, piece), lane(source)]
         return pltpu.make_async_remote_copy(
             src_ref=at, dst_ref=at,
-            send_sem=ysend.at[way, step - 1, k], recv_sem=yrcv.at[way, step - 1, k],
-            device_id=ypeer(sign), device_id_type=MESH,
+            send_sem=ysend.at[way, leg, k], recv_sem=yrcv.at[way, leg, k],
+            device_id=ypeer(sign * (1 + leg % 2)), device_id_type=MESH,
         )
 
-    waited = set()
-
-    def ring_wait(way, step, k):
-        if (way, step, k) not in waited:
-            waited.add((way, step, k))
-            ring(way, step, k).wait_recv()
-
-    def ring_step(step, p):
-        for k in range(p * CUT, (p + 1) * CUT):
-            for way in range(2):
-                if step == half and skips(way, k):
-                    continue
-                if step > 1:
-                    ring_wait(way, step - 1, k)
-                ring(way, step, k).start()
-                pending.append(ring(way, step, k).wait_send)
-
-    def ring_end(p):
-        for step in range(1, half + 1):
-            for k in range(p * CUT, (p + 1) * CUT):
-                for way in range(2):
-                    if not (step == half and skips(way, k)):
-                        ring_wait(way, step, k)
+    def start(copy):
+        copy.start()
+        pending.append(copy.wait_send)
 
     for p in range(2):
         landed(recv4.at[p, pl.ds(1, ndp - 1)], 6 + p)
         full[p, :, mine] = nn(pack, recv4[p].reshape(slots, LANE)).astype(BF)
-        ring_step(1, p)
-    for step in range(2, half + 1):
-        for p in range(2):
-            ring_step(step, p)
-    ring_end(0)
+        for leg in (1, 0):
+            for k, way in pieces(p):
+                start(hop(way, leg, k))
+    for p in range(2):
+        for k, way in pieces(p):
+            hop(way, 1, k).wait_recv()
+            if way == k % 2:
+                start(hop(way, 3, k))
+            start(hop(way, 2, k))
+
+    def gather_end(p):
+        for k, way in pieces(p):
+            hop(way, 0, k).wait_recv()
+            hop(way, 2, k).wait_recv()
+            if way == k % 2:
+                hop(way, 3, k).wait_recv()
+
+    gather_end(0)
 
     for copy in fetch[4:]:
         copy.wait()
@@ -246,47 +239,60 @@
     hidden = (active * lift).astype(BF)
     own[0] = nn(hidden, w_down[...])
 
-    def pass_on(way, step, k):
+    def block(p, k, to):
+        return own[p, pl.ds(k % CUT * piece, piece), lane(to)]
+
+    def pass_on(way, leg, k):
         sign = 1 if way == 0 else -1
         return pltpu.make_async_remote_copy(
-            src_ref=ystage.at[way, step - 1, k], dst_ref=yrecv.at[way, step - 1, k],
-            send_sem=psend.at[way, step - 1, k], recv_sem=prcv.at[way, step - 1, k],
-            device_id=ypeer(sign), device_id_type=MESH,
+            src_ref=ystage.at[way, leg, k], dst_ref=yrecv.at[way, leg, k],
+            send_sem=psend.at[way, leg, k], recv_sem=prcv.at[way, leg, k],
+            device_id=ypeer(sign * (1 + leg % 2)), device_id_type=MESH,
         )
 
-    def pass_step(step, p):
-        for k in range(p * CUT, (p + 1) * CUT):
-            for way in range(2):
-                sign = 1 if way == 0 else -1
-                if step == 1 and skips(way, k):
-                    continue
-                value = own[p, pl.ds(k % CUT * piece, piece), lane(y + sign * (half + 1 - step))]
-                if step > 2 or (step == 2 and not skips(way, k)):
-                    pass_on(way, step - 1, k).wait_recv()
-                    value = value + yrecv[way, step - 2, k].astype(F32)
-                ystage[way, step - 1, k] = value.astype(BF)
-                pass_on(way, step, k).start()
-                pending.append(pass_on(way, step, k).wait_send)
+    def pass_first(p):
+        for k, way in pieces(p):
+            sign = 1 if way == 0 else -1
+            if way == k % 2:
+                ystage[way, 3, k] = block(p, k, y + 4 * sign).astype(BF)
+                start(pass_on(way, 3, k))
+            ystage[way, 2, k] = block(p, k, y + 3 * sign).astype(BF)
+            start(pass_on(way, 2, k))
+        for k, way in pieces(p):
+            sign = 1 if way == 0 else -1
+            ystage[way, 0, k] = block(p, k, y + sign).astype(BF)
+            start(pass_on(way, 0, k))
+
+    def pass_second(p):
+        for k, way in pieces(p):
+            sign = 1 if way == 0 else -1
+            value = block(p, k, y + 2 * sign)
+            pass_on(way, 2, k).wait_recv()
+            value = value + yrecv[way, 2, k].astype(F32)
+            if way == k % 2:
+                pass_on(way, 3, k).wait_recv()
+                value = value + yrecv[way, 3, k].astype(F32)
+            ystage[way, 1, k] = value.astype(BF)
+            start(pass_on(way, 1, k))
 
     def pass_end(p):
         parts = []
         for k in range(p * CUT, (p + 1) * CUT):
-            value = own[p, pl.ds(k % CUT * piece, piece), lane(y)]
+            value = block(p, k, y)
             for way in range(2):
-                if half == 1 and skips(way, k):
-                    continue
-                pass_on(way, half, k).wait_recv()
-                value = value + yrecv[way, half - 1, k].astype(F32)
+                for leg in (0, 1):
+                    pass_on(way, leg, k).wait_recv()
+                    value = value + yrecv[way, leg, k].astype(F32)
             parts.append(value.astype(BF))
         return jnp.concatenate(parts, axis=0)
 
-    pass_step(1, 0)
-    ring_end(1)
+    pass_first(0)
+    gather_end(1)
     hidden_grad = nt(full[1], w_down[...])
     gate_grad = (hidden_grad * lift * (sigma * (1.0 + gate * (1.0 - sigma)))).astype(BF)
     lift_grad = (hidden_grad * active).astype(BF)
     own[1] = nt(gate_grad, w_gate[...]) + nt(lift_grad, w_up[...])
-    pass_step(1, 1)
+    pass_first(1)
     work = [
         (gate_out, hbm_gate_out, lambda: tn(full[0], gate_grad)),
         (lift_out, hbm_lift_out, lambda: tn(full[0], lift_grad)),
@@ -300,13 +306,11 @@
         copy.start()
         pending.append(copy.wait)
 
-    for step in range(2, half + 1):
-        pass_step(step, 0)
-        pass_step(step, 1)
-        if work:
-            do_work()
-    while work:
-        do_work()
+    pass_second(0)
+    do_work()
+    pass_second(1)
+    do_work()
+    do_work()
 
     for p in range(2):
         back[p] = nn(unpack, pass_end(p)).astype(BF).reshape(ndp, PAD, LANE)
@@ -359,17 +363,22 @@
     finish()
 
 
-def hand_over(*refs):
-    count = (len(refs) - 2) // 3
+def hand_over(count, *refs):
     given, outs, held = refs[:count], refs[count:2 * count], refs[2 * count:3 * count]
     arrived, left = refs[3 * count:]
-    ins = [pltpu.make_async_copy(given[n], held[n], arrived.at[n]) for n in range(count)]
-    out = [pltpu.make_async_copy(held[n], outs[n], left.at[n]) for n in range(count)]
+    ins, out = [], []
+    for n in range(count):
+        rows = given[n].shape[0]
+        step = min(rows, 128 * 1024 // given[n].shape[1])
+        for at in range(0, rows, step):
+            part, k = pl.ds(at, step), len(ins)
+            ins.append(pltpu.make_async_copy(given[n].at[part], held[n].at[part], arrived.at[k]))
+            out.append(pltpu.make_async_copy(held[n].at[part], outs[n].at[part], left.at[k]))
     for copy in ins:
         copy.start()
-    for n in range(count):
-        ins[n].wait()
-        out[n].start()
+    for here, copy in zip(ins, out):
+        here.wait()
+        copy.start()
     for copy in out:
         copy.wait()
 
@@ -433,12 +442,12 @@
             ),
         )(tokens, routes.T, scores.T, down, up, w_gate, w_up, w_down, cot)
         layer_out, token_grad, down_grad, up_grad, gate_out, lift_out, dexp_out = pl.pallas_call(
-            hand_over,
+            functools.partial(hand_over, len(outs)),
             out_shape=[shape(out.shape, out.dtype) for out in outs],
             in_specs=[outside] * len(outs),
             out_specs=[outside] * len(outs),
             scratch_shapes=[vm(*out.shape, kind=out.dtype) for out in outs] + [
-                pltpu.SemaphoreType.DMA((len(outs),)), pltpu.SemaphoreType.DMA((len(outs),)),
+                pltpu.SemaphoreType.DMA((16,)), pltpu.SemaphoreType.DMA((16,)),
             ],
             compiler_params=pltpu.CompilerParams(vmem_limit_bytes=58 * 1024 * 1024),
         )(*outs)

time: 109 us -> 105 us (0.963)
  Pallas kernels: 108 us -> 104 us
    pallas_call x1, Pallas kernels: 106 us -> 102 us  [local(): pl.pallas_call(functools.partial(kernel, ndp, nz, ny), out_shape=(shape((...]
where the time goes in v3:
time: 105 us
  Pallas kernels  104 us (99%)
    pallas_call x1, Pallas kernels, local(): pl.pallas_call(functools.partial(kernel, ndp, nz, ny), out_shape=(shape((...  102 us
    pallas_call x1, Pallas kernels, local(): pl.pallas_call(functools.partial(hand_over, len(outs)), out_shape=[shape(...  2.45 us

profile of v3, /device:TPU:1, one launch (start us, length us, event | category | flops | bytes accessed | tf_op | source)
XLA Modules:
  0.0 104.9 jit_solution(3974005841731720376)
XLA Ops:
  0.6 101.8 %shard_map.144 = (bf16[112,128]{1,0:T(8,128)(2,1)}, bf16[112,128]{1,0:T(8,128)(2,1)}, f32[64,112]{1,0:T(8,128)}, f32[64,112]{1,0:T(8,128)}, bf16[1024,256]{1,0:T...) custom-call(bf16[112,128]{1,0:T(8,128)(2,1)} %bitcast.9, s32[4,128]{1,0:T(4,128)} %bitcast.11, ...), custom_call_target="tpu_custom_call" | custom-call | tf_op jit(solution)/shard_map/pallas_call | solution.py:405
  102.5 2.4 %shard_map.145 = (bf16[112,128]{1,0:T(8,128)(2,1)}, bf16[112,128]{1,0:T(8,128)(2,1)}, f32[64,112]{1,0:T(8,128)}, f32[64,112]{1,0:T(8,128)}, bf16[1024,256]{1,0:T...) custom-call(bf16[112,128]{1,0:T(8,128)(2,1)} %get-tuple-element.21.refs_0_, ...), custom_call_target="tpu_custom_call" | custom-call | tf_op jit(solution)/shard_map/pallas_call | solution.py:444

commit v4 on v3

--- a/solution.py
+++ b/solution.py
@@ -211,10 +211,13 @@
     for p in range(2):
         landed(recv4.at[p, pl.ds(1, ndp - 1)], 6 + p)
         full[p, :, mine] = nn(pack, recv4[p].reshape(slots, LANE)).astype(BF)
-        for leg in (1, 0):
+        for leg in ((1, 0), (1,))[p]:
             for k, way in pieces(p):
                 start(hop(way, leg, k))
     for p in range(2):
+        if p == 1:
+            for k, way in pieces(p):
+                start(hop(way, 0, k))
         for k, way in pieces(p):
             hop(way, 1, k).wait_recv()
             if way == k % 2:

time: 105 us -> 104 us (level)
  no operation moved by 1% of the time
where the time goes in v4:
time: 104 us
  Pallas kernels  103 us (99%)
    pallas_call x1, Pallas kernels, local(): pl.pallas_call(functools.partial(kernel, ndp, nz, ny), out_shape=(shape((...  101 us
    pallas_call x1, Pallas kernels, local(): pl.pallas_call(functools.partial(hand_over, len(outs)), out_shape=[shape(...  2.45 us

profile of v4, /device:TPU:1, one launch (start us, length us, event | category | flops | bytes accessed | tf_op | source)
XLA Modules:
  0.0 104.0 jit_solution(9787218821790350706)
XLA Ops:
  0.6 100.9 %shard_map.144 = (bf16[112,128]{1,0:T(8,128)(2,1)}, bf16[112,128]{1,0:T(8,128)(2,1)}, f32[64,112]{1,0:T(8,128)}, f32[64,112]{1,0:T(8,128)}, bf16[1024,256]{1,0:T...) custom-call(bf16[112,128]{1,0:T(8,128)(2,1)} %bitcast.9, s32[4,128]{1,0:T(4,128)} %bitcast.11, ...), custom_call_target="tpu_custom_call" | custom-call | tf_op jit(solution)/shard_map/pallas_call | solution.py:408
  101.5 2.4 %shard_map.145 = (bf16[112,128]{1,0:T(8,128)(2,1)}, bf16[112,128]{1,0:T(8,128)(2,1)}, f32[64,112]{1,0:T(8,128)}, f32[64,112]{1,0:T(8,128)}, bf16[1024,256]{1,0:T...) custom-call(bf16[112,128]{1,0:T(8,128)(2,1)} %get-tuple-element.21.refs_0_, ...), custom_call_target="tpu_custom_call" | custom-call | tf_op jit(solution)/shard_map/pallas_call | solution.py:447
